TPU v7x, 32 devices: a whole 2x2x4 slice. The times are simulated.
32 devices in a mesh: blk: 8 (over y, x, core), exp: 4 (over z).
Axes of the slice: x: 2, y: 2, z: 4, core: 2. Of those that a mesh axis runs over, the one named last changes fastest.
Arguments:
- residual_deposit_sequence: bfloat16 [4, 1024, 1536], P('exp', 'blk'), may hold values from -60 to 60
- premix_rescaler: float32 [1536], replicated, may hold values from 0.25 to 1.75
- asking_projector: bfloat16 [1536, 1536], P(None, 'exp'), may hold values from -0.15625 to 0.15625
- lookup_projector: bfloat16 [1536, 512], P(None, 'exp'), may hold values from -0.15625 to 0.15625
- content_projector: bfloat16 [1536, 512], P(None, 'exp'), may hold values from -0.15625 to 0.15625
- final_projector: bfloat16 [1536, 1536], P('exp'), may hold values from -0.15625 to 0.15625
- logit_multipliers: float32 [12], replicated, may hold values from 1.5 to 6
- premixture_rescaler: float32 [1536], replicated, may hold values from 0.25 to 1.75
- specialist_switch_tensor: bfloat16 [8, 1536, 384], P('exp'), may hold values from -0.15625 to 0.15625
- specialist_widen_tensor: bfloat16 [8, 1536, 384], P('exp'), may hold values from -0.15625 to 0.15625
- specialist_shrink_tensor: bfloat16 [8, 384, 1536], P('exp'), may hold values from -0.3125 to 0.3125
- picked_specialist_labels: int32 [4, 1024, 2], P(None, 'blk'), may hold values from 0 to 7, all different within a row; in each aligned block of 128 rows (0 to 127, 128 to 255, ..., all dimensions but the last counted through in order) at most 64 rows name the same one
- specialist_shares: float32 [4, 1024, 2], P(None, 'blk'), may hold values from 0.1 to 1
Outputs:
- attention_update: bfloat16 [4, 1024, 1536], P('exp', 'blk')
- expert_update: bfloat16 [4, 1024, 1536], P('exp', 'blk')
Inputs may be any that keep to these rules, and one draw needn't show every extreme that they name: `picked_specialist_labels`: the 2 ids of a hit differ. Within each event's 128 hits on one index of blk (an aligned block of 128 rows) no expert is named by more than 64 hits, a bound that some block reaches.
All inputs are finite; a program needn't handle non-finite values.
Results may differ from a plain program's by a relative error of at most 0.019.
Values may be sent and summed in bfloat16 or wider, within the bound.
A program may use at most 192 MiB of HBM per device.

v0:
```python
import math
import jax
import jax.numpy as jnp
from jax import lax
from jax.sharding import PartitionSpec as P

D = 1536
PER_LANE_DIM = 128
TOP = 2
CAP = 64


def norm_rows(values, norm_gain):
    widened = values.astype(jnp.float32)
    return (
        widened * lax.rsqrt(jnp.mean(widened * widened, axis=-1, keepdims=True) + 1e-05) * norm_gain
    )


def head_norm(values):
    return values * lax.rsqrt(jnp.mean(values * values, axis=-1, keepdims=True) + 1e-06)


def attend_hits(
    rescaled_entries,
    asking_projector,
    lookup_projector,
    content_projector,
    final_projector,
    logit_multipliers,
):
    events, row_count, model_width = rescaled_entries.shape
    common_key_heads = lookup_projector.shape[1] // PER_LANE_DIM
    local_lane_count = asking_projector.shape[1] // PER_LANE_DIM
    askers_per_lookup = local_lane_count // common_key_heads
    query_heads = jnp.einsum(
        "std,de->ste", rescaled_entries, asking_projector, preferred_element_type=jnp.float32
    )
    query_heads = head_norm(
        query_heads.reshape(events, row_count, common_key_heads, askers_per_lookup, PER_LANE_DIM)
    ).astype(jnp.bfloat16)
    key_heads = jnp.einsum(
        "std,de->ste", rescaled_entries, lookup_projector, preferred_element_type=jnp.float32
    )
    key_heads = head_norm(
        key_heads.reshape(events, row_count, common_key_heads, PER_LANE_DIM)
    ).astype(jnp.bfloat16)
    value_heads = jnp.einsum(
        "std,de->ste", rescaled_entries, content_projector, preferred_element_type=jnp.float32
    )
    value_heads = value_heads.reshape(events, row_count, common_key_heads, PER_LANE_DIM).astype(
        jnp.bfloat16
    )
    inverse_root_dim = (logit_multipliers / math.sqrt(PER_LANE_DIM)).reshape(
        common_key_heads, askers_per_lookup
    )
    key_piece = lax.all_gather(key_heads, "blk", axis=1, tiled=True)
    value_piece = lax.all_gather(value_heads, "blk", axis=1, tiled=True)
    scores = jnp.einsum(
        "sikgd,sjkd->skgij", query_heads, key_piece, preferred_element_type=jnp.float32
    )
    expo = jnp.exp(scores * inverse_root_dim[None, :, :, None, None])
    totals = jnp.sum(expo, axis=-1)
    mixture = jnp.einsum(
        "skgij,sjkd->skgid",
        expo.astype(jnp.bfloat16),
        value_piece,
        preferred_element_type=jnp.float32,
    )
    totals, mixture = (totals, mixture)
    heads_out = head_norm(mixture / totals[..., None]).astype(jnp.bfloat16)
    out_blocks = final_projector.reshape(
        common_key_heads, askers_per_lookup, PER_LANE_DIM, model_width
    )
    return jnp.einsum("skgid,kgde->sie", heads_out, out_blocks, preferred_element_type=jnp.float32)


def slot_tables(chosen, expert_count):
    events, row_count, top_count = chosen.shape
    flat_ids = chosen.reshape(events, row_count * top_count)
    onehot = (
        flat_ids[:, :, None] == jnp.arange(expert_count, dtype=jnp.int32)[None, None, :]
    ).astype(jnp.int32)
    before = jnp.cumsum(onehot, axis=1) - onehot
    slot_of = jnp.sum(before * onehot, axis=2)
    source_rows = jnp.arange(row_count * top_count, dtype=jnp.int32)[None, :] // top_count
    event_index = jnp.arange(events, dtype=jnp.int32)[:, None]
    tables = (
        jnp.zeros((events, expert_count, CAP), jnp.int32)
        .at[event_index, flat_ids, slot_of]
        .set(source_rows)
    )
    return (slot_of, tables)


def run_experts(
    batched, specialist_switch_tensor, specialist_widen_tensor, specialist_shrink_tensor
):
    gate_act = jnp.einsum(
        "sjcd,jdf->sjcf", batched, specialist_switch_tensor, preferred_element_type=jnp.float32
    )
    up_act = jnp.einsum(
        "sjcd,jdf->sjcf", batched, specialist_widen_tensor, preferred_element_type=jnp.float32
    )
    hidden = (jax.nn.silu(gate_act) * up_act).astype(jnp.bfloat16)
    return jnp.einsum(
        "sjcf,jfd->sjcd", hidden, specialist_shrink_tensor, preferred_element_type=jnp.float32
    ).astype(jnp.bfloat16)


def body(
    residual_deposit_sequence,
    premix_rescaler,
    asking_projector,
    lookup_projector,
    content_projector,
    final_projector,
    logit_multipliers,
    premixture_rescaler,
    specialist_switch_tensor,
    specialist_widen_tensor,
    specialist_shrink_tensor,
    picked_specialist_labels,
    specialist_shares,
):
    specialist_slot = lax.axis_index("exp")
    exp_count = lax.axis_size("exp")
    rows_all = lax.all_gather(residual_deposit_sequence, "exp", axis=0, tiled=True)
    rescaled_entries = norm_rows(rows_all, premix_rescaler).astype(jnp.bfloat16)
    local_lane_count = asking_projector.shape[1] // PER_LANE_DIM
    device_scratch = lax.dynamic_slice_in_dim(
        logit_multipliers, specialist_slot * local_lane_count, local_lane_count
    )
    partial_out = attend_hits(
        rescaled_entries,
        asking_projector,
        lookup_projector,
        content_projector,
        final_projector,
        device_scratch,
    )
    attention_full = lax.psum_scatter(
        partial_out.astype(jnp.bfloat16), "exp", scatter_dimension=0, tiled=True
    ).astype(jnp.float32)
    attention_update = attention_full.astype(jnp.bfloat16)
    residual = residual_deposit_sequence.astype(jnp.float32) + attention_full
    expert_in = norm_rows(residual, premixture_rescaler).astype(jnp.bfloat16)
    row_count = expert_in.shape[1]
    local_experts = specialist_switch_tensor.shape[0]
    expert_count = local_experts * exp_count
    own_ids = lax.dynamic_slice_in_dim(picked_specialist_labels, specialist_slot, 1, 0)
    own_gates = lax.dynamic_slice_in_dim(specialist_shares, specialist_slot, 1, 0).reshape(
        row_count * TOP
    )
    slot_of, tables = slot_tables(own_ids, expert_count)
    outgoing = jnp.take(expert_in[0], tables[0].reshape(expert_count * CAP), axis=0)
    outgoing = outgoing.reshape(exp_count, local_experts, CAP, D)
    produced = run_experts(
        lax.all_to_all(outgoing, "exp", split_axis=0, concat_axis=0, tiled=True),
        specialist_switch_tensor,
        specialist_widen_tensor,
        specialist_shrink_tensor,
    )
    returned = lax.all_to_all(produced, "exp", split_axis=0, concat_axis=0, tiled=True)
    position = own_ids.reshape(row_count * TOP) * CAP + slot_of[0]
    values = jnp.take(returned.reshape(expert_count * CAP, D), position, axis=0).astype(jnp.float32)
    combined = jnp.sum((values * own_gates[:, None]).reshape(row_count, TOP, D), axis=1)
    expert_update = combined.astype(jnp.bfloat16)[None]
    return (attention_update, expert_update)


def solution(mesh):
    placed = (
        P("exp", "blk", None),
        P(),
        P(None, "exp"),
        P(None, "exp"),
        P(None, "exp"),
        P("exp", None),
        P(),
        P(),
        P("exp", None, None),
        P("exp", None, None),
        P("exp", None, None),
        P(None, "blk", None),
        P(None, "blk", None),
    )
    return jax.shard_map(
        body,
        mesh=mesh,
        in_specs=placed,
        out_specs=(P("exp", "blk", None), P("exp", "blk", None)),
        check_vma=False,
    )
```

profile of v0, /device:TPU:0, one launch (start us, length us, event | category | flops | bytes accessed | tf_op | source)
XLA Modules:
  0.0 258.9 jit_solution(3094345826512784104)
XLA Ops:
  7.2 0.0 copy-start
  7.2 0.0 copy-start.7
  7.2 0.0 all-gather.6.cloned.1.call-start
  7.2 0.7 all-gather.6.cloned.1.call-update
  7.9 0.0 all-gather.8.cloned.1.call-start
  8.0 41.4 %all-gather.6.cloned.1.call-done = bf16[4,128,1536]{2,1,0:T(8,128)(2,1)} async-done(((bf16[1,128,1536]{2,1,0:T(8,128)(2,1)}), bf16[4,128,1536]{2,1,0:T(8,128)(2,1)}) %all-gather.6.cloned.1.call-update) | async-done | bytes 1572880 | tf_op jit(solution)/shard_map/all_gather | solution.py:128
  49.4 1.9 fusion.1
  51.4 0.0 copy-start.8
  51.4 0.0 copy-start.9
  51.4 1.5 multiply_reduce_fusion.3
  52.9 0.7 multiply_convert_fusion.5
  53.6 0.0 all-gather.8.cloned.1.call-update
  53.6 0.0 copy-start.10
  53.6 0.0 all-gather.10.cloned.1.call-start
  53.7 2.7 %convolution_convert_fusion.1 = bf16[4,128,128]{2,1,0:T(8,128)(2,1)} fusion(bf16[4,128,1536]{2,1,0:T(8,128)(2,1)} %all-gather.6.cloned.1.call-done, f32[1536]{0:T(1024)S(1)} %copy-done.9, f32[4,128]{1,0:T(4,128)S(1)} %add_rsqrt_fusion.3, bf16[1536,128]{1,0:T(8,128)(2,1)S(1)} %copy-done.8), kind=kOutput, calls=%fused_computation.35 | convolution fusion | flops 204537856 | bytes 2105344 | tf_op jit(solution)/shard_map/std,de->ste/dot_general | solution.py:48
  56.4 0.0 all-gather.10.cloned.1.call-update
  56.4 0.0 reduce-scatter.2.cloned.1.call-start
  56.5 0.1 dynamic-slice_multiply_fusion
  56.6 3.7 %fusion.70 = (f32[4,128,384]{2,1,0:T(8,128)S(1)}, f32[4,128,384]{2,1,0:T(8,128)}) fusion(bf16[1536,384]{1,0:T(8,128)(2,1)} %param.15, bf16[4,128,1536]{2,1,0:T(8,128)(2,1)} %all-gather.6.cloned.1.call-done, f32[1536]{0:T(1024)S(1)} %copy-done.9, f32[4,128]{1,0:T(4,128)S(1)} %add_rsqrt_fusion.3), kind=kOutput, calls=%fused_computation.101 | convolution fusion | flops 607322112 | bytes 4333568 | tf_op jit(solution)/shard_map/std,de->ste/dot_general | solution.py:36
  60.2 1.1 copy.53
  61.4 1.4 copy.52
  62.8 1.2 reduce_sum.80
  64.0 12.2 %all-gather.8.cloned.1.call-done = bf16[4,1024,128]{1,2,0:T(8,128)(2,1)} async-done(((bf16[4,128,128]{1,2,0:T(8,128)(2,1)}), bf16[4,1024,128]{1,2,0:T(8,128)(2,1)}) %all-gather.8.cloned.1.call-update) | async-done | bytes 1048592 | tf_op jit(solution)/shard_map/all_gather | solution.py:57
  76.2 5.4 %bitcast_reduce_fusion = (f32[4,3,128]{2,1,0:T(4,128)S(1)}, f32[4,1024,128,3]{2,1,3,0:T(8,128)}) fusion(f32[3]{0:T(128)S(1)} %dynamic-slice_multiply_fusion, f32[4,128,3,128]{1,3,2,0:T(8,128)S(1)} %bitcast.150, f32[4,128,3]{1,2,0:T(4,128)S(1)} %add_rsqrt_fusion.1, bf16[4,1024,128]{1,2,0:T(8,128)(2,1)} %all-gather.8.cloned.1.call-done), kind=kOutput, calls=%fused_computation.3 | convolution fusion | flops 406190592 | bytes 8138764 | tf_op jit(solution)/shard_map/sikgd,sjkd->skgij/dot_general | solution.py:59
  81.6 20.6 %all-gather.10.cloned.1.call-done = bf16[4,1024,128]{2,1,0:T(8,128)(2,1)} async-done(((bf16[4,128,128]{2,1,0:T(8,128)(2,1)}), bf16[4,1024,128]{2,1,0:T(8,128)(2,1)}) %all-gather.10.cloned.1.call-update) | async-done | bytes 1048592 | tf_op jit(solution)/shard_map/all_gather | solution.py:58
  102.2 4.4 %multiply_reduce_fusion.2 = (f32[4,3,128]{2,1,0:T(4,128)S(1)}, f32[4,3,128,128]{2,3,1,0:T(8,128)S(1)}) fusion(f32[4,3,128]{2,1,0:T(4,128)S(1)} %get-tuple-element.8, bf16[4,1024,128]{2,1,0:T(8,128)(2,1)} %all-gather.10.cloned.1.call-done, f32[4,1024,128,3]{2,1,3,0:T(8,128)} %get-tuple-element.9, f32[3]{0:T(128)S(1)} %dynamic-slice_multiply_fusion), kind=kOutput, calls=%fused_computation.50 | convolution fusion | flops 406387200 | bytes 8138764 | tf_op jit(solution)/shard_map/skgij,sjkd->skgid/dot_general | solution.py:64
  106.7 0.0 copy-done.4
  106.7 2.2 fusion.8
  108.9 0.0 reduce-scatter.2.cloned.1.call-update
  108.9 0.0 copy-start.1
  108.9 0.7 broadcast_multiply_fusion
  109.7 0.1 copy.59
  109.8 0.1 eq.27
  109.9 0.1 reshape.479
  110.0 0.0 copy-start.5
  110.1 0.6 reduce-window.6
  110.7 0.2 slice_reduce_fusion
  110.9 0.1 fusion.67
  111.1 11.2 %scatter_fusion = s32[8,64]{1,0:T(8,128)S(1)} fusion(s32[8,64]{1,0:T(8,128)S(1)} %broadcast.318, s32[256]{0:T(256)S(1)} %bitcast.148, s32[256]{0:T(256)S(1)} %bitcast.159), kind=kCustom, calls=%fused_computation.2 | custom fusion | bytes 5120 | tf_op jit(solution)/shard_map/scatter | solution.py:91
  122.3 0.1 reshape_squeeze.6
  122.4 22.0 %reduce-scatter.2.cloned.1.call-done = bf16[1,128,1536]{2,1,0:T(8,128)(2,1)} async-done(((bf16[4,128,1536]{2,1,0:T(8,128)(2,1)}), bf16[1,128,1536]{2,1,0:T(8,128)(2,1)}) %reduce-scatter.2.cloned.1.call-update) | async-done | bytes 393232 | tf_op jit(solution)/shard_map/reduce_scatter | solution.py:142
  144.3 0.0 copy-done.1
  144.3 1.2 multiply_reduce_fusion.1
  145.6 1.2 fusion.60
  146.7 3.0 %gather_fusion = bf16[512,1536]{1,0:T(8,128)(2,1)} fusion(bf16[128,1536]{1,0:T(8,128)(2,1)S(1)} %fusion.60, s32[1024]{0:T(1024)S(1)} %pad_clamp_fusion.1), kind=kCustom, calls=%fused_computation | custom fusion | bytes 3147776 | tf_op jit(solution)/shard_map/jit(_take)/gather | solution.py:156
  149.7 1.6 broadcast_select_fusion
  151.3 0.0 copy-start.6
  151.3 39.7 %all_to_all.10 = bf16[4,2,64,1536]{3,2,1,0:T(8,128)(2,1)S(1)} all-to-all(bf16[4,2,64,1536]{3,2,1,0:T(8,128)(2,1)S(1)} %broadcast_select_fusion), channel_id=1, replica_groups=mesh['blk'=8,'exp'=4] {'exp'}, dimensions={0} | all-to-all | bytes 3145728 | tf_op jit(solution)/shard_map/all_to_all | solution.py:159
  191.0 1.1 copy-done.3
  192.1 1.0 fusion.17
  193.2 5.1 %fusion.9 = bf16[4,2,64,1536]{3,2,0,1:T(8,128)(2,1)} fusion(bf16[2,384,1536]{2,1,0:T(8,128)(2,1)S(1)} %copy-done, bf16[2,1536,384]{2,1,0:T(8,128)(2,1)} %param.22, bf16[4,2,64,1536]{3,2,1,0:T(8,128)(2,1)} %copy-done.3, f32[4,2,64,384]{3,2,0,1:T(8,128)S(1)} %fusion.17), kind=kOutput, calls=%fused_computation.18 | convolution fusion | flops 1209925632 | bytes 8650752 | tf_op jit(solution)/shard_map/sjcf,jfd->sjcd/dot_general | solution.py:106
  198.3 2.7 %copy.65 = bf16[4,2,64,1536]{3,2,1,0:T(8,128)(2,1)} copy(bf16[4,2,64,1536]{3,2,0,1:T(8,128)(2,1)} %fusion.9) | data formatting | bytes 3145728 | tf_op jit(solution)/shard_map/convert_element_type | solution.py:108
  200.9 4.3 %all-to-all-start.1 = ((bf16[4,2,64,1536]{3,2,1,0:T(8,128)(2,1)}), bf16[4,2,64,1536]{3,2,1,0:T(8,128)(2,1)}, u32[]{:S(2)}, u32[]{:S(2)}) async-start(bf16[4,2,64,1536]{3,2,1,0:T(8,128)(2,1)} %copy.65), calls=%async_computation.2 | async-start | bytes 3145728 | tf_op jit(solution)/shard_map/all_to_all | solution.py:164
  205.3 0.1 reduce_sum.84
  205.4 0.1 copy.66
  205.5 0.1 mul.173
  205.7 0.7 dynamic-slice_bitcast_fusion
  206.3 0.1 copy.67
  206.5 0.1 copy.60
  206.5 0.1 copy.61
  206.7 35.1 %all-to-all-done.1 = bf16[4,2,64,1536]{3,2,1,0:T(8,128)(2,1)} async-done(((bf16[4,2,64,1536]{3,2,1,0:T(8,128)(2,1)}), bf16[4,2,64,1536]{3,2,1,0:T(8,128)(2,1)}, u32[]{:S(2)}, u32[]{:S(2)}) %all-to-all-start.1) | async-done | bytes 1572896 | tf_op jit(solution)/shard_map/all_to_all | solution.py:164
  241.8 4.5 %gather_fusion.1 = bf16[256,1536]{1,0:T(8,128)(2,1)} fusion(bf16[512,1536]{1,0:T(8,128)(2,1)} %bitcast.38, s32[1024]{0:T(1024)S(1)} %pad_clamp_fusion), kind=kCustom, calls=%fused_computation.1 | custom fusion | bytes 1573888 | tf_op jit(solution)/shard_map/jit(_take)/gather | solution.py:166
  246.3 2.2 gather.15
  248.4 3.9 %multiply_reduce_fusion = bf16[128,1536]{1,0:T(8,128)(2,1)} fusion(bf16[128,2,1536]{2,1,0:T(2,128)(2,1)S(1)} %gather.15, pred[128,2]{1,0:T(8,128)(4,1)S(1)} %copy.61, f32[128,2]{1,0:T(8,128)S(1)} %copy.67), kind=kLoop, calls=%fused_computation.24 | loop fusion | flops 1376256 | bytes 1180928 | tf_op jit(solution)/shard_map/reduce_sum | solution.py:167
  (31 shorter events, 0.2 us)
Async XLA Ops:
  7.2 186.0 %copy-start = (bf16[2,384,1536]{2,1,0:T(8,128)(2,1)S(1)}, bf16[2,384,1536]{2,1,0:T(8,128)(2,1)}, u32[]{:S(2)}) copy-start(bf16[2,384,1536]{2,1,0:T(8,128)(2,1)} %param.23) | copy-start | bytes 7077892
  7.2 44.2 %copy-start.7 = (bf16[1536,128]{1,0:T(8,128)(2,1)S(1)}, bf16[1536,128]{1,0:T(8,128)(2,1)}, u32[]{:S(2)}) copy-start(bf16[1536,128]{1,0:T(8,128)(2,1)} %param.16) | copy-start | bytes 1179652
  7.2 42.2 %all-gather.6.cloned.1.call-start = ((), (), s32[]{:S(2)}) async-start(), calls=%async_computation.3 | async-start | bytes 1966080 | tf_op jit(solution)/shard_map/all_gather | solution.py:128
  7.9 68.3 %all-gather.8.cloned.1.call-start = ((), (), s32[]{:S(2)}) async-start(), calls=%async_computation.5 | async-start | bytes 1179648 | tf_op jit(solution)/shard_map/all_gather | solution.py:57
  49.4 1.9 copy-start.2
  51.4 2.3 copy-start.8
  51.4 2.3 copy-start.9
  53.6 2.9 %copy-start.10 = (f32[12]{0:T(128)S(1)}, f32[12]{0:T(128)}, u32[]{:S(2)}) copy-start(f32[12]{0:T(128)} %param.19) | copy-start | bytes 148
  53.6 48.6 %all-gather.10.cloned.1.call-start = ((), (), s32[]{:S(2)}) async-start(), calls=%async_computation.6 | async-start | bytes 1179648 | tf_op jit(solution)/shard_map/all_gather | solution.py:58
  56.4 87.9 %reduce-scatter.2.cloned.1.call-start = ((), (), s32[]{:S(2)}) async-start(), calls=%async_computation.4 | async-start | bytes 1966080 | tf_op jit(solution)/shard_map/reduce_scatter | solution.py:142
  102.2 4.5 %copy-start.4 = (bf16[384,1536]{1,0:T(8,128)(2,1)S(1)}, bf16[384,1536]{1,0:T(8,128)(2,1)}, u32[]{:S(2)}) copy-start(bf16[384,1536]{1,0:T(8,128)(2,1)} %param.18) | copy-start | bytes 3538948
  108.9 35.4 %copy-start.1 = (bf16[1,128,1536]{2,1,0:T(8,128)(2,1)S(1)}, bf16[1,128,1536]{2,1,0:T(8,128)(2,1)}, u32[]{:S(2)}) copy-start(bf16[1,128,1536]{2,1,0:T(8,128)(2,1)} %param.13) | copy-start | bytes 1179652
  110.0 35.5 %copy-start.5 = (f32[1536]{0:T(1024)S(1)}, f32[1536]{0:T(1024)}, u32[]{:S(2)}) copy-start(f32[1536]{0:T(1024)} %param.20) | copy-start | bytes 18436
  151.3 40.8 %copy-start.6 = (bf16[2,1536,384]{2,1,0:T(8,128)(2,1)S(1)}, bf16[2,1536,384]{2,1,0:T(8,128)(2,1)}, u32[]{:S(2)}) copy-start(bf16[2,1536,384]{2,1,0:T(8,128)(2,1)} %param.21) | copy-start | bytes 7077892
  191.0 1.1 copy-start.3
  200.9 40.9 %all-to-all-start.1 = ((bf16[4,2,64,1536]{3,2,1,0:T(8,128)(2,1)}), bf16[4,2,64,1536]{3,2,1,0:T(8,128)(2,1)}, u32[]{:S(2)}, u32[]{:S(2)}) async-start(bf16[4,2,64,1536]{3,2,1,0:T(8,128)(2,1)} %copy.65), calls=%async_computation.2 | async-start | bytes 3145728 | tf_op jit(solution)/shard_map/all_to_all | solution.py:164
Sparse Core Ops, SparseCore 0:
  9.6 39.7 all-gather.5
  53.8 22.4 all-gather.7
  78.7 23.4 all-gather.9
  109.0 35.2 reduce-scatter.1
where the time goes:
time: 260 us; the launch traced here: 259 us
  waiting for transfers between devices  132 us (51%)
  blocking collectives  39.7 us (15%)
  local copies, waits for them, and re-layouts  29.3 us (11%)
  matrix products  26 us (10%)
  between operations  14.1 us (5%)
  other arithmetic  13.3 us (5%)
  starting transfers between devices  4.49 us (2%)
    all_gather x1, waiting for transfers between devices, body(): lax.all_gather(residual_deposit_sequence, 'exp', axis=0, tiled=True)  41.4 us
    all_to_all x1, blocking collectives, body(): lax.all_to_all(outgoing, 'exp', split_axis=0, concat_axis=0, tiled=True)  39.7 us
    all_to_all x1, waiting for transfers between devices, body(): lax.all_to_all(produced, 'exp', split_axis=0, concat_axis=0, tiled=True)  35.1 us
    reduce_scatter x1, waiting for transfers between devices, body(): lax.psum_scatter(partial_out.astype(jnp.bfloat16), 'exp', scatter_dimensi...  22 us
    all_gather x1, waiting for transfers between devices, attend_hits(): value_piece = lax.all_gather(value_heads, 'blk', axis=1, tiled=True)  20.6 us
    all_gather x1, waiting for transfers between devices, attend_hits(): key_piece = lax.all_gather(key_heads, 'blk', axis=1, tiled=True)  12.2 us
    scatter x1, local copies, waits for them, and re-layouts, slot_tables(): tables = jnp.zeros((events, expert_count, CAP), jnp.int32).at[event_index...  11.2 us
    gather x2, local copies, waits for them, and re-layouts, body(): jnp.take(returned.reshape(expert_count * CAP, D), position, axis=0)  6.65 us
  transfers between devices with their start and end apart: 5, of which 5 were waited for; matrix products, arithmetic and copies ran while one was open for 12% of the time, Pallas kernels for 0%

commit v1 on v0

--- a/solution.py
+++ b/solution.py
@@ -54,8 +54,13 @@
     inverse_root_dim = (logit_multipliers / math.sqrt(PER_LANE_DIM)).reshape(
         common_key_heads, askers_per_lookup
     )
-    key_piece = lax.all_gather(key_heads, "blk", axis=1, tiled=True)
-    value_piece = lax.all_gather(value_heads, "blk", axis=1, tiled=True)
+    key_piece, value_piece = jnp.split(
+        lax.all_gather(
+            jnp.concatenate([key_heads, value_heads], axis=0), "blk", axis=1, tiled=True
+        ),
+        [key_heads.shape[0]],
+        axis=0,
+    )
     scores = jnp.einsum(
         "sikgd,sjkd->skgij", query_heads, key_piece, preferred_element_type=jnp.float32
     )

time: 260 us -> 239 us (0.919)
  waiting for transfers between devices: 132 us -> 119 us
  matrix products: 26 us -> 18.6 us
    all_gather x2 -> x1, waiting for transfers between devices: 32.8 us -> 19.6 us  [attend_hits(): lax.all_gather(jnp.concatenate([key_heads, value_heads], axis=0), 'blk',...]
    dot_general x1, matrix products: 4.44 us -> 1.44 us  [attend_hits(): jnp.einsum('skgij,sjkd->skgid', expo.astype(jnp.bfloat16), value_piece, p...]
  transfers between devices with their start and end apart: 5 -> 4, of which waited for: 5 -> 4; matrix products, arithmetic and copies ran while one was open for 12% -> 9% of each run, Pallas kernels for 0% -> 0%
where the time goes in v1:
time: 239 us; the launch traced here: 238 us
  waiting for transfers between devices  119 us (50%)
  blocking collectives  39.7 us (17%)
  local copies, waits for them, and re-layouts  29.3 us (12%)
  matrix products  18.6 us (8%)
  between operations  14.1 us (6%)
  other arithmetic  13.4 us (6%)
  starting transfers between devices  4.45 us (2%)
    all_gather x1, waiting for transfers between devices, body(): lax.all_gather(residual_deposit_sequence, 'exp', axis=0, tiled=True)  41.4 us
    all_to_all x1, blocking collectives, body(): lax.all_to_all(outgoing, 'exp', split_axis=0, concat_axis=0, tiled=True)  39.7 us
    all_to_all x1, waiting for transfers between devices, body(): lax.all_to_all(produced, 'exp', split_axis=0, concat_axis=0, tiled=True)  35.1 us
    reduce_scatter x1, waiting for transfers between devices, body(): lax.psum_scatter(partial_out.astype(jnp.bfloat16), 'exp', scatter_dimensi...  22 us
    all_gather x1, waiting for transfers between devices, attend_hits(): lax.all_gather(jnp.concatenate([key_heads, value_heads], axis=0), 'blk',...  19.6 us
    scatter x1, local copies, waits for them, and re-layouts, slot_tables(): tables = jnp.zeros((events, expert_count, CAP), jnp.int32).at[event_index...  11.2 us
    gather x2, local copies, waits for them, and re-layouts, body(): jnp.take(returned.reshape(expert_count * CAP, D), position, axis=0)  6.65 us
    dot_general x1, matrix products, run_experts(): jnp.einsum('sjcf,jfd->sjcd', hidden, specialist_shrink_tensor, preferred_...  5.1 us
  transfers between devices with their start and end apart: 4, of which 4 were waited for; matrix products, arithmetic and copies ran while one was open for 9% of the time, Pallas kernels for 0%

profile of v1, /device:TPU:0, one launch (start us, length us, event | category | flops | bytes accessed | tf_op | source)
XLA Modules:
  0.0 238.3 jit_solution(12476343048516355148)
XLA Ops:
  7.2 0.0 copy-start
  7.2 0.0 copy-start.8
  7.2 0.0 all-gather.3.cloned.1.call-start
  7.2 0.7 all-gather.3.cloned.1.call-update
  7.9 0.0 all-gather.5.cloned.1.call-start
  8.0 41.4 %all-gather.3.cloned.1.call-done = bf16[4,128,1536]{2,1,0:T(8,128)(2,1)} async-done(((bf16[1,128,1536]{2,1,0:T(8,128)(2,1)}), bf16[4,128,1536]{2,1,0:T(8,128)(2,1)}) %all-gather.3.cloned.1.call-update) | async-done | bytes 1572880 | tf_op jit(solution)/shard_map/all_gather | solution.py:133
  49.4 1.9 fusion.1
  51.3 0.0 copy-done.8
  51.4 0.0 copy-start.9
  51.4 0.0 copy-start.10
  51.4 1.5 multiply_reduce_fusion.3
  53.0 0.0 copy-start.11
  53.0 0.8 fusion.39
  53.8 0.7 pad_maximum_fusion
  54.5 0.0 all-gather.5.cloned.1.call-update
  54.5 0.0 reduce-scatter.2.cloned.1.call-start
  54.6 0.1 dynamic-slice_multiply_fusion
  54.7 3.7 %fusion.68 = (f32[4,128,384]{2,1,0:T(8,128)S(1)}, f32[4,128,384]{2,1,0:T(8,128)}) fusion(bf16[1536,384]{1,0:T(8,128)(2,1)} %param.15, bf16[4,128,1536]{2,1,0:T(8,128)(2,1)} %all-gather.3.cloned.1.call-done, f32[1536]{0:T(1024)S(1)} %copy-done.10, f32[4,128]{1,0:T(4,128)S(1)} %add_rsqrt_fusion.3), kind=kOutput, calls=%fused_computation.104 | convolution fusion | flops 607322112 | bytes 4333568 | tf_op jit(solution)/shard_map/std,de->ste/dot_general | solution.py:36
  58.3 1.2 copy.56
  59.5 1.4 copy.55
  60.9 1.2 reduce_sum.80
  62.2 19.6 %all-gather.5.cloned.1.call-done = bf16[8,1024,1,128]{1,3,0,2:T(8,128)(2,1)} async-done(((bf16[8,128,1,128]{1,3,0,2:T(8,128)(2,1)}), bf16[8,1024,1,128]{1,3,0,2:T(8,128)(2,1)}) %all-gather.5.cloned.1.call-update) | async-done | bytes 2097168 | tf_op jit(solution)/shard_map/all_gather | solution.py:58
  81.7 3.0 %bitcast_reduce_fusion = (f32[4,3,128]{2,1,0:T(4,128)S(1)}, f32[4,1024,128,3]{2,1,3,0:T(8,128)S(1)}) fusion(f32[3]{0:T(128)S(1)} %dynamic-slice_multiply_fusion, f32[4,128,3,128]{1,3,2,0:T(8,128)S(1)} %bitcast.156, f32[4,128,3]{1,2,0:T(4,128)S(1)} %add_rsqrt_fusion.1, bf16[8,1024,1,128]{1,3,0,2:T(8,128)(2,1)} %all-gather.5.cloned.1.call-done), kind=kOutput, calls=%fused_computation.3 | convolution fusion | flops 406190592 | bytes 8138764 | tf_op jit(solution)/shard_map/sikgd,sjkd->skgij/dot_general | solution.py:64
  84.7 0.0 copy-done.5
  84.7 0.0 copy-start.4
  84.7 1.4 multiply_reduce_fusion.2
  86.2 2.2 fusion.8
  88.4 0.0 reduce-scatter.2.cloned.1.call-update
  88.4 0.0 copy-start.1
  88.4 0.7 broadcast_multiply_fusion
  89.1 0.1 copy.61
  89.3 0.1 eq.27
  89.4 0.1 reshape.479
  89.5 0.0 copy-start.6
  89.6 0.6 reduce-window.6
  90.1 0.2 slice_reduce_fusion
  90.4 0.1 fusion.65
  90.6 11.2 %scatter_fusion = s32[8,64]{1,0:T(8,128)S(1)} fusion(s32[8,64]{1,0:T(8,128)S(1)} %broadcast.318, s32[256]{0:T(256)S(1)} %bitcast.154, s32[256]{0:T(256)S(1)} %bitcast.165), kind=kCustom, calls=%fused_computation.2 | custom fusion | bytes 5120 | tf_op jit(solution)/shard_map/scatter | solution.py:96
  101.8 0.1 reshape_squeeze.6
  101.9 22.0 %reduce-scatter.2.cloned.1.call-done = bf16[1,128,1536]{2,1,0:T(8,128)(2,1)} async-done(((bf16[4,128,1536]{2,1,0:T(8,128)(2,1)}), bf16[1,128,1536]{2,1,0:T(8,128)(2,1)}) %reduce-scatter.2.cloned.1.call-update) | async-done | bytes 393232 | tf_op jit(solution)/shard_map/reduce_scatter | solution.py:147
  123.8 1.2 multiply_reduce_fusion.1
  125.1 0.0 copy-done.6
  125.1 1.2 fusion.57
  126.2 3.0 %gather_fusion = bf16[512,1536]{1,0:T(8,128)(2,1)} fusion(bf16[128,1536]{1,0:T(8,128)(2,1)S(1)} %fusion.57, s32[1024]{0:T(1024)S(1)} %pad_clamp_fusion.1), kind=kCustom, calls=%fused_computation | custom fusion | bytes 3147776 | tf_op jit(solution)/shard_map/jit(_take)/gather | solution.py:161
  129.2 1.6 broadcast_select_fusion
  130.8 0.0 copy-start.7
  130.8 39.7 %all_to_all.10 = bf16[4,2,64,1536]{3,2,1,0:T(8,128)(2,1)S(1)} all-to-all(bf16[4,2,64,1536]{3,2,1,0:T(8,128)(2,1)S(1)} %broadcast_select_fusion), channel_id=1, replica_groups=mesh['blk'=8,'exp'=4] {'exp'}, dimensions={0} | all-to-all | bytes 3145728 | tf_op jit(solution)/shard_map/all_to_all | solution.py:164
  170.5 1.1 copy-done.3
  171.6 1.0 fusion.17
  172.6 0.0 copy-done
  172.6 5.1 %fusion.9 = bf16[4,2,64,1536]{3,2,0,1:T(8,128)(2,1)} fusion(bf16[2,384,1536]{2,1,0:T(8,128)(2,1)S(1)} %copy-done, bf16[2,1536,384]{2,1,0:T(8,128)(2,1)} %param.22, bf16[4,2,64,1536]{3,2,1,0:T(8,128)(2,1)} %copy-done.3, f32[4,2,64,384]{3,2,0,1:T(8,128)S(1)} %fusion.17), kind=kOutput, calls=%fused_computation.18 | convolution fusion | flops 1209925632 | bytes 8650752 | tf_op jit(solution)/shard_map/sjcf,jfd->sjcd/dot_general | solution.py:111
  177.7 2.7 %copy.67 = bf16[4,2,64,1536]{3,2,1,0:T(8,128)(2,1)} copy(bf16[4,2,64,1536]{3,2,0,1:T(8,128)(2,1)} %fusion.9) | data formatting | bytes 3145728 | tf_op jit(solution)/shard_map/convert_element_type | solution.py:113
  180.4 4.3 %all-to-all-start.1 = ((bf16[4,2,64,1536]{3,2,1,0:T(8,128)(2,1)}), bf16[4,2,64,1536]{3,2,1,0:T(8,128)(2,1)}, u32[]{:S(2)}, u32[]{:S(2)}) async-start(bf16[4,2,64,1536]{3,2,1,0:T(8,128)(2,1)} %copy.67), calls=%async_computation.2 | async-start | bytes 3145728 | tf_op jit(solution)/shard_map/all_to_all | solution.py:169
  184.7 0.1 reduce_sum.84
  184.9 0.1 copy.68
  185.0 0.1 mul.173
  185.1 0.1 copy.62
  185.2 0.1 copy.63
  185.4 0.7 dynamic-slice_bitcast_fusion
  186.1 0.1 copy.69
  186.2 35.1 %all-to-all-done.1 = bf16[4,2,64,1536]{3,2,1,0:T(8,128)(2,1)} async-done(((bf16[4,2,64,1536]{3,2,1,0:T(8,128)(2,1)}), bf16[4,2,64,1536]{3,2,1,0:T(8,128)(2,1)}, u32[]{:S(2)}, u32[]{:S(2)}) %all-to-all-start.1) | async-done | bytes 1572896 | tf_op jit(solution)/shard_map/all_to_all | solution.py:169
  221.3 4.5 %gather_fusion.1 = bf16[256,1536]{1,0:T(8,128)(2,1)} fusion(bf16[512,1536]{1,0:T(8,128)(2,1)} %bitcast.43, s32[1024]{0:T(1024)S(1)} %pad_clamp_fusion), kind=kCustom, calls=%fused_computation.1 | custom fusion | bytes 1573888 | tf_op jit(solution)/shard_map/jit(_take)/gather | solution.py:171
  225.8 2.2 gather.15
  227.9 3.9 %multiply_reduce_fusion = bf16[128,1536]{1,0:T(8,128)(2,1)} fusion(bf16[128,2,1536]{2,1,0:T(2,128)(2,1)S(1)} %gather.15, pred[128,2]{1,0:T(8,128)(4,1)S(1)} %copy.63, f32[128,2]{1,0:T(8,128)S(1)} %copy.69), kind=kLoop, calls=%fused_computation.24 | loop fusion | flops 1376256 | bytes 1180928 | tf_op jit(solution)/shard_map/reduce_sum | solution.py:172
  (31 shorter events, 0.2 us)
Async XLA Ops:
  7.2 165.5 %copy-start = (bf16[2,384,1536]{2,1,0:T(8,128)(2,1)S(1)}, bf16[2,384,1536]{2,1,0:T(8,128)(2,1)}, u32[]{:S(2)}) copy-start(bf16[2,384,1536]{2,1,0:T(8,128)(2,1)} %param.23) | copy-start | bytes 7077892
  7.2 44.2 %copy-start.8 = (bf16[1536,128]{1,0:T(8,128)(2,1)S(1)}, bf16[1536,128]{1,0:T(8,128)(2,1)}, u32[]{:S(2)}) copy-start(bf16[1536,128]{1,0:T(8,128)(2,1)} %param.16) | copy-start | bytes 1179652
  7.2 42.2 %all-gather.3.cloned.1.call-start = ((), (), s32[]{:S(2)}) async-start(), calls=%async_computation.3 | async-start | bytes 1966080 | tf_op jit(solution)/shard_map/all_gather | solution.py:133
  7.9 73.8 %all-gather.5.cloned.1.call-start = ((), (), s32[]{:S(2)}) async-start(), calls=%async_computation.4 | async-start | bytes 2359296 | tf_op jit(solution)/shard_map/all_gather | solution.py:58
  49.4 1.9 copy-start.2
  51.4 1.6 copy-start.9
  51.4 1.6 copy-start.10
  53.0 1.6 copy-start.11
  54.5 69.3 %reduce-scatter.2.cloned.1.call-start = ((), (), s32[]{:S(2)}) async-start(), calls=%async_computation.5 | async-start | bytes 1966080 | tf_op jit(solution)/shard_map/reduce_scatter | solution.py:147
  81.7 3.0 %copy-start.5 = (bf16[8,1024,1,128]{1,3,0,2:T(8,128)(2,1)S(1)}, bf16[8,1024,1,128]{1,3,0,2:T(8,128)(2,1)}, u32[]{:S(2)}) copy-start(bf16[8,1024,1,128]{1,3,0,2:T(8,128)(2,1)} %all-gather.5.cloned.1.call-done) | copy-start | bytes 6291460
  84.7 1.5 copy-start.4
  88.4 35.4 %copy-start.1 = (bf16[1,128,1536]{2,1,0:T(8,128)(2,1)S(1)}, bf16[1,128,1536]{2,1,0:T(8,128)(2,1)}, u32[]{:S(2)}) copy-start(bf16[1,128,1536]{2,1,0:T(8,128)(2,1)} %param.13) | copy-start | bytes 1179652
  89.5 35.5 %copy-start.6 = (f32[1536]{0:T(1024)S(1)}, f32[1536]{0:T(1024)}, u32[]{:S(2)}) copy-start(f32[1536]{0:T(1024)} %param.20) | copy-start | bytes 18436
  130.8 40.8 %copy-start.7 = (bf16[2,1536,384]{2,1,0:T(8,128)(2,1)S(1)}, bf16[2,1536,384]{2,1,0:T(8,128)(2,1)}, u32[]{:S(2)}) copy-start(bf16[2,1536,384]{2,1,0:T(8,128)(2,1)} %param.21) | copy-start | bytes 7077892
  170.5 1.1 copy-start.3
  180.4 40.9 %all-to-all-start.1 = ((bf16[4,2,64,1536]{3,2,1,0:T(8,128)(2,1)}), bf16[4,2,64,1536]{3,2,1,0:T(8,128)(2,1)}, u32[]{:S(2)}, u32[]{:S(2)}) async-start(bf16[4,2,64,1536]{3,2,1,0:T(8,128)(2,1)} %copy.67), calls=%async_computation.2 | async-start | bytes 3145728 | tf_op jit(solution)/shard_map/all_to_all | solution.py:169
Sparse Core Ops, SparseCore 0:
  9.6 39.7 all-gather.2
  54.6 27.0 all-gather.4
  88.5 35.2 reduce-scatter.1
